TPU v7x, 32 devices: a whole 2x2x4 slice. The times are simulated.
32 devices in a mesh: groups: 2 (over y), ep: 4 (over z), tp: 4 (over x, core).
Axes of the slice: x: 2, y: 2, z: 4, core: 2. Of those that a mesh axis runs over, the one named last changes fastest.
Arguments:
- queries: bfloat16 [256, 8192], P(('groups', 'ep'), 'tp'), parts along dimension 0, may hold values from -4.5 to 4.5
- cached_key_table: bfloat16 [256, 128, 512], P(('groups', 'ep'), None, 'tp'), parts along dimension 0, may hold values from -4.5 to 4.5
- cached_value_table: bfloat16 [256, 128, 512], P(('groups', 'ep'), None, 'tp'), parts along dimension 0, may hold values from -10 to 10
- fresh_token_keys: bfloat16 [256, 512], P(('groups', 'ep'), 'tp'), parts along dimension 0, may hold values from -4.5 to 4.5
- fresh_token_values: bfloat16 [256, 512], P(('groups', 'ep'), 'tp'), parts along dimension 0, may hold values from -10 to 10
- cache_len: int32 [256], P(('groups', 'ep')), parts along dimension 0, may hold values from 1 to 128, as said below
- out_proj: bfloat16 [8192, 4096], P('tp', 'ep'), may hold values from -0.0625 to 0.0625
- residual: bfloat16 [256, 4096], P(('groups', 'ep'), 'tp'), parts along dimension 0, may hold values from -10.5 to 10.5
- norm_gain: bfloat16 [4096], replicated, may hold values from 0.099609375 to 1.8984375
- routes: int32 [256, 8], P(('groups', 'ep')), parts along dimension 0, may hold values from 0 to 7, as said below
- gate_weights: float32 [256, 8], P(('groups', 'ep')), parts along dimension 0, may hold values from 0.05 to 0.4
- gate_proj: bfloat16 [8, 768, 4096], P('ep', 'tp'), may hold values from -0.09375 to 0.09375
- up_proj: bfloat16 [8, 768, 4096], P('ep', 'tp'), may hold values from -0.09375 to 0.09375
- down_proj: bfloat16 [8, 768, 4096], P('ep', 'tp'), may hold values from -0.21875 to 0.21875
Outputs:
- layer_out: bfloat16 [256, 4096], P(('groups', 'ep'), 'tp'), parts along dimension 0
There are 2 independent parts, one for each index of `groups`. A program takes and returns all parts, laid end to end along the dimension named above; an argument that names none is the same for every part. Nothing has to cross between parts.
Inputs may be any that keep to these rules, and one draw needn't show every extreme that they name: Row r uses the cache positions below cache_len[r]; some row uses all 128. `routes`: each row names 8 different experts. Among the rows of one ep index no expert is named more than 32 times, and one expert, the same for every ep index, is named exactly 32 times by the rows of each index.
All inputs are finite; a program needn't handle non-finite values.
Results may differ from a plain program's by a relative error of at most 0.008.
Values may be sent and summed in bfloat16 or wider, within the bound.
A program may use at most 128 MiB of HBM per device.

v0:
```python
import math

import jax
import jax.numpy as jnp
from jax import lax
from jax.sharding import PartitionSpec as P

HEAD_DIM = 128
TOP = 8


def attend_local(
    queries, cached_key_table, cached_value_table, fresh_token_keys, fresh_token_values, cache_len
):
    rows_here = queries.shape[0]
    kv_heads = cached_key_table.shape[2] // HEAD_DIM
    query_group_width = queries.shape[1] // HEAD_DIM // kv_heads
    cache_size = cached_key_table.shape[1]
    query_block = queries.reshape(rows_here, kv_heads, query_group_width, HEAD_DIM)
    key_block = cached_key_table.reshape(rows_here, cache_size, kv_heads, HEAD_DIM)
    value_block = cached_value_table.reshape(rows_here, cache_size, kv_heads, HEAD_DIM)
    newkey_block = fresh_token_keys.reshape(rows_here, kv_heads, HEAD_DIM)
    newval_block = fresh_token_values.reshape(rows_here, kv_heads, HEAD_DIM)
    score_scale = 1.0 / math.sqrt(HEAD_DIM)
    scores = (
        jnp.einsum("rkgd,rjkd->rkgj", query_block, key_block, preferred_element_type=jnp.float32)
        * score_scale
    )
    own_score = (
        jnp.einsum("rkgd,rkd->rkg", query_block, newkey_block, preferred_element_type=jnp.float32)
        * score_scale
    )
    usable = jnp.arange(cache_size, dtype=jnp.int32)[None, :] < cache_len[:, None]
    scores = jnp.where(usable[:, None, None, :], scores, -jnp.inf)
    highest = jnp.maximum(jnp.max(scores, axis=-1), own_score)
    exp_scores = jnp.exp(scores - highest[..., None])
    own_exp = jnp.exp(own_score - highest)
    denominator = jnp.sum(exp_scores, axis=-1) + own_exp
    attn_probs = (exp_scores / denominator[..., None]).astype(jnp.bfloat16)
    own_prob = (own_exp / denominator).astype(jnp.bfloat16)
    attended = jnp.einsum(
        "rkgj,rjkd->rkgd", attn_probs, value_block, preferred_element_type=jnp.float32
    )
    attended = (
        attended
        + own_prob.astype(jnp.float32)[..., None] * newval_block.astype(jnp.float32)[:, :, None, :]
    )
    return attended.reshape(rows_here, -1).astype(jnp.bfloat16)


def per_device(
    queries,
    cached_key_table,
    cached_value_table,
    fresh_token_keys,
    fresh_token_values,
    cache_len,
    out_proj,
    residual,
    norm_gain,
    routes,
    gate_weights,
    gate_proj,
    up_proj,
    down_proj,
):
    attended = attend_local(
        queries,
        cached_key_table,
        cached_value_table,
        fresh_token_keys,
        fresh_token_values,
        cache_len,
    )
    partial_all = jnp.dot(
        lax.all_gather(attended, "ep", axis=0, tiled=True),
        out_proj,
        preferred_element_type=jnp.float32,
    )
    partial_rows = lax.all_to_all(partial_all, "ep", split_axis=0, concat_axis=1, tiled=True)
    ep_count = lax.axis_size("ep")
    tp_index = lax.axis_index("tp")
    rows_here = residual.shape[0]
    col_width = residual.shape[1]
    local_experts = gate_proj.shape[0]
    expert_count = local_experts * ep_count
    capacity = min(rows_here, 2 * rows_here * TOP // expert_count)
    flat_routes = routes.reshape(-1)
    pair_count = flat_routes.shape[0]
    member = (flat_routes[:, None] == jnp.arange(expert_count, dtype=jnp.int32)[None, :]).astype(
        jnp.int32
    )
    earlier = jnp.cumsum(member, axis=0) - member
    position = jnp.sum(earlier * member, axis=1)
    target = flat_routes * capacity + position
    slot_match = (
        jnp.arange(expert_count * capacity, dtype=jnp.int32)[:, None] == target[None, :]
    ).astype(jnp.int32)
    occupied = jnp.sum(slot_match, axis=1)
    source_row = jnp.sum(
        slot_match * (jnp.arange(pair_count, dtype=jnp.int32) // TOP)[None, :], axis=1
    )
    gain_full = norm_gain.astype(jnp.float32)
    own_cols = lax.dynamic_slice_in_dim(
        partial_rows, tp_index * col_width, col_width, 1
    ) + residual.astype(jnp.float32)
    with_residual = lax.dynamic_update_slice_in_dim(partial_rows, own_cols, tp_index * col_width, 1)
    hidden_full = lax.psum(with_residual, "tp")
    mean_square = jnp.mean(hidden_full * hidden_full, axis=-1, keepdims=True)
    normed = (hidden_full * lax.rsqrt(mean_square + 1e-06) * gain_full).astype(jnp.bfloat16)
    hidden = lax.dynamic_slice_in_dim(hidden_full, tp_index * col_width, col_width, 1)
    picked = jnp.where(occupied[:, None] > 0, normed[source_row], jnp.zeros((), normed.dtype))
    arrived = lax.all_to_all(
        picked.reshape(ep_count, local_experts, capacity, normed.shape[1]),
        "ep",
        split_axis=0,
        concat_axis=0,
        tiled=True,
    )
    gate_part = jnp.einsum("aesd,efd->aesf", arrived, gate_proj, preferred_element_type=jnp.float32)
    up_part = jnp.einsum("aesd,efd->aesf", arrived, up_proj, preferred_element_type=jnp.float32)
    activated = (jax.nn.silu(gate_part) * up_part).astype(jnp.bfloat16)
    partial_out = jnp.einsum(
        "aesf,efd->aesd", activated, down_proj, preferred_element_type=jnp.float32
    )
    reduced = lax.psum_scatter(
        partial_out.astype(jnp.bfloat16), "tp", scatter_dimension=3, tiled=True
    ).astype(jnp.float32)
    returned = lax.all_to_all(
        reduced.astype(jnp.bfloat16), "ep", split_axis=0, concat_axis=0, tiled=True
    ).astype(reduced.dtype)
    flat_back = returned.reshape(expert_count * capacity, col_width)
    pair_out = flat_back[target].reshape(rows_here, TOP, col_width)
    mixture = jnp.sum(gate_weights[:, :, None] * pair_out, axis=1)
    return (hidden + mixture).astype(jnp.bfloat16)


def solution(mesh):
    return jax.shard_map(
        per_device,
        mesh=mesh,
        in_specs=(
            P(("groups", "ep"), "tp"),
            P(("groups", "ep"), None, "tp"),
            P(("groups", "ep"), None, "tp"),
            P(("groups", "ep"), "tp"),
            P(("groups", "ep"), "tp"),
            P(("groups", "ep")),
            P("tp", "ep"),
            P(("groups", "ep"), "tp"),
            P(),
            P(("groups", "ep"), None),
            P(("groups", "ep"), None),
            P("ep", "tp", None),
            P("ep", "tp", None),
            P("ep", "tp", None),
        ),
        out_specs=P(("groups", "ep"), "tp"),
        check_vma=False,
    )
```

profile of v0, /device:TPU:0, one launch (start us, length us, event | category | flops | bytes accessed | tf_op | source)
XLA Modules:
  0.0 220.2 jit_solution(10238340907117745675)
XLA Ops:
  6.5 0.0 copy-start
  6.5 0.0 copy-start.5
  6.5 1.1 copy.47
  7.6 0.7 iota_compare_fusion.1
  8.4 0.9 fusion.44
  9.2 0.0 copy-start.2
  9.2 2.1 fusion.52
  11.4 0.2 fusion.40
  11.6 0.0 copy-done.5
  11.7 1.7 fusion.29
  13.4 17.4 %all_gather.3 = bf16[128,2048]{1,0:T(8,128)(2,1)S(1)} all-gather(bf16[32,2048]{1,0:T(8,128)(2,1)S(1)} %bitcast.80), channel_id=1, replica_groups=mesh['groups'=2,'ep'=4,'tp'=4] {'ep'}, dimensions={0}, use_global_device_ids=true | all-gather | bytes 655360 | tf_op jit(solution)/shard_map/all_gather | solution.py:76
  30.8 0.0 copy-done.2
  30.8 0.0 copy-start.4
  30.8 0.0 copy-start.6
  30.8 1.5 fusion.53
  32.3 0.0 copy-start.3
  32.3 5.5 %all-to-all-start = ((f32[4,32,1024]{2,1,0:T(8,128)}), f32[4,32,1024]{2,1,0:T(8,128)}, u32[]{:S(2)}, u32[]{:S(2)}) async-start(f32[4,32,1024]{2,1,0:T(8,128)} %bitcast.77), calls=%async_computation | async-start | bytes 1048576 | tf_op jit(solution)/shard_map/all_to_all | solution.py:80
  37.8 0.0 all-reduce.2.cloned.1.call-start
  37.8 0.0 copy-done.4
  37.8 0.1 copy.35
  37.9 0.1 eq.40
  38.0 0.1 reshape.202
  38.1 0.0 copy-done.6
  38.1 0.6 reduce-window.6
  38.7 0.2 slice_reduce_fusion
  39.0 0.1 copy.40
  39.0 0.1 mul.118
  39.2 0.1 fusion.48
  39.2 0.2 convert_reduce_fusion
  39.4 0.1 gt.18
  39.5 10.4 %all-to-all-done = f32[4,32,1024]{2,1,0:T(8,128)} async-done(((f32[4,32,1024]{2,1,0:T(8,128)}), f32[4,32,1024]{2,1,0:T(8,128)}, u32[]{:S(2)}, u32[]{:S(2)}) %all-to-all-start) | async-done | bytes 524320 | tf_op jit(solution)/shard_map/all_to_all | solution.py:80
  50.0 1.9 copy.46
  51.9 0.0 copy-done.3
  51.9 1.6 add_dynamic-update-slice_fusion
  53.4 0.0 all-reduce.2.cloned.1.call-update
  53.4 0.0 reduce-scatter.2.cloned.1.call-start
  53.5 32.4 %all-reduce.2.cloned.1.call-done = f32[32,4096]{1,0:T(8,128)} async-done(((f32[32,4096]{1,0:T(8,128)}), f32[32,4096]{1,0:T(8,128)}) %all-reduce.2.cloned.1.call-update) | async-done | bytes 524304 | tf_op jit(solution)/shard_map/psum | solution.py:108
  85.9 1.2 multiply_reduce_fusion
  87.1 1.2 multiply_convert_fusion
  88.2 3.2 %gather_fusion = bf16[256,4096]{1,0:T(8,128)(2,1)} fusion(bf16[32,4096]{1,0:T(8,128)(2,1)S(1)} %multiply_convert_fusion, s32[1024]{0:T(1024)S(1)} %pad_clamp_fusion.1), kind=kCustom, calls=%fused_computation | custom fusion | bytes 4195328 | tf_op jit(solution)/shard_map/gather | solution.py:112
  91.4 1.8 broadcast_select_fusion
  93.2 0.0 copy-start.8
  93.2 51.9 %all_to_all.29 = bf16[4,2,32,4096]{3,2,1,0:T(8,128)(2,1)S(1)} all-to-all(bf16[4,2,32,4096]{3,2,1,0:T(8,128)(2,1)S(1)} %broadcast_select_fusion), channel_id=1, replica_groups=mesh['groups'=2,'ep'=4,'tp'=4] {'ep'}, dimensions={0} | all-to-all | bytes 4194304 | tf_op jit(solution)/shard_map/all_to_all | solution.py:113
  145.2 0.0 copy-start.1
  145.2 1.3 copy-done.1
  146.5 0.0 copy-done.8
  146.5 1.2 fusion.8
  147.7 0.0 copy-done
  147.7 5.7 %fusion = bf16[4,2,32,4096]{3,2,0,1:T(8,128)(2,1)} fusion(bf16[2,192,4096]{2,1,0:T(8,128)(2,1)S(1)} %copy-done, bf16[2,192,4096]{2,1,0:T(8,128)(2,1)} %param.26, bf16[4,2,32,4096]{3,2,1,0:T(8,128)(2,1)} %copy-done.1, f32[4,2,32,192]{3,2,0,1:T(8,128)S(1)} %fusion.8), kind=kOutput, calls=%fused_computation.3 | convolution fusion | flops 806649856 | bytes 10682368 | tf_op jit(solution)/shard_map/aesf,efd->aesd/dot_general | solution.py:123
  153.4 0.0 copy-start.7
  153.4 0.0 reduce-scatter.2.cloned.1.call-update
  153.4 29.8 %reduce-scatter.2.cloned.1.call-done = bf16[4,2,32,1024]{3,2,0,1:T(8,128)(2,1)} async-done(((bf16[4,2,32,4096]{3,2,0,1:T(8,128)(2,1)}), bf16[4,2,32,1024]{3,2,0,1:T(8,128)(2,1)}) %reduce-scatter.2.cloned.1.call-update) | async-done | bytes 524304 | tf_op jit(solution)/shard_map/reduce_scatter | solution.py:126
  183.2 1.9 copy.39
  185.1 4.6 %all-to-all-start.2 = ((bf16[4,2,32,1024]{3,2,1,0:T(8,128)(2,1)}), bf16[4,2,32,1024]{3,2,1,0:T(8,128)(2,1)}, u32[]{:S(2)}, u32[]{:S(2)}) async-start(bf16[4,2,32,1024]{3,2,1,0:T(8,128)(2,1)} %copy.39), calls=%async_computation.3 | async-start | bytes 1048576 | tf_op jit(solution)/shard_map/all_to_all | solution.py:129
  189.7 0.0 copy-done.7
  189.7 0.1 copy.34
  189.8 14.5 %all-to-all-done.2 = bf16[4,2,32,1024]{3,2,1,0:T(8,128)(2,1)} async-done(((bf16[4,2,32,1024]{3,2,1,0:T(8,128)(2,1)}), bf16[4,2,32,1024]{3,2,1,0:T(8,128)(2,1)}, u32[]{:S(2)}, u32[]{:S(2)}) %all-to-all-start.2) | async-done | bytes 524320 | tf_op jit(solution)/shard_map/all_to_all | solution.py:129
  204.3 2.1 bitcast_convert_fusion
  206.4 3.8 %gather_fusion.1 = f32[256,1024]{1,0:T(8,128)} fusion(f32[256,1024]{1,0:T(8,128)} %bitcast_convert_fusion, s32[1024]{0:T(1024)S(1)} %pad_clamp_fusion), kind=kCustom, calls=%fused_computation.1 | custom fusion | bytes 2098176 | tf_op jit(solution)/shard_map/gather | solution.py:133
  210.2 1.6 fusion.30
  211.8 1.6 add_convert_fusion
  (16 shorter events, 0.2 us)
Async XLA Ops:
  6.5 141.1 %copy-start = (bf16[2,192,4096]{2,1,0:T(8,128)(2,1)S(1)}, bf16[2,192,4096]{2,1,0:T(8,128)(2,1)}, u32[]{:S(2)}) copy-start(bf16[2,192,4096]{2,1,0:T(8,128)(2,1)} %param.27) | copy-start | bytes 9437188
  6.5 5.1 %copy-start.5 = (bf16[32,128]{1,0:T(8,128)(2,1)S(1)}, bf16[32,128]{1,0:T(8,128)(2,1)}, u32[]{:S(2)}) copy-start(bf16[32,128]{1,0:T(8,128)(2,1)} %param.18) | copy-start | bytes 24580
  9.2 21.5 %copy-start.2 = (bf16[2048,1024]{1,0:T(8,128)(2,1)S(1)}, bf16[2048,1024]{1,0:T(8,128)(2,1)}, u32[]{:S(2)}) copy-start(bf16[2048,1024]{1,0:T(8,128)(2,1)} %param.20) | copy-start | bytes 12582916
  30.8 7.1 %copy-start.4 = (s32[32,8]{0,1:T(8,128)S(1)}, s32[32,8]{0,1:T(8,128)}, u32[]{:S(2)}) copy-start(s32[32,8]{0,1:T(8,128)} %param.23) | copy-start | bytes 3076
  30.8 7.3 %copy-start.6 = (bf16[4096]{0:T(1024)(128)(2,1)S(1)}, bf16[4096]{0:T(1024)(128)(2,1)}, u32[]{:S(2)}) copy-start(bf16[4096]{0:T(1024)(128)(2,1)} %param.22) | copy-start | bytes 24580
  32.3 19.6 %copy-start.3 = (bf16[32,1024]{1,0:T(8,128)(2,1)S(1)}, bf16[32,1024]{1,0:T(8,128)(2,1)}, u32[]{:S(2)}) copy-start(bf16[32,1024]{1,0:T(8,128)(2,1)} %param.21) | copy-start | bytes 196612
  32.3 17.7 %all-to-all-start = ((f32[4,32,1024]{2,1,0:T(8,128)}), f32[4,32,1024]{2,1,0:T(8,128)}, u32[]{:S(2)}, u32[]{:S(2)}) async-start(f32[4,32,1024]{2,1,0:T(8,128)} %bitcast.77), calls=%async_computation | async-start | bytes 1048576 | tf_op jit(solution)/shard_map/all_to_all | solution.py:80
  37.8 48.1 %all-reduce.2.cloned.1.call-start = ((), (), s32[]{:S(2)}) async-start(), calls=%async_computation.4 | async-start | bytes 1048576 | tf_op jit(solution)/shard_map/psum | solution.py:108
  53.4 129.7 %reduce-scatter.2.cloned.1.call-start = ((), (), s32[]{:S(2)}) async-start(), calls=%async_computation.5 | async-start | bytes 2621440 | tf_op jit(solution)/shard_map/reduce_scatter | solution.py:126
  93.2 53.2 %copy-start.8 = (bf16[2,192,4096]{2,1,0:T(8,128)(2,1)S(1)}, bf16[2,192,4096]{2,1,0:T(8,128)(2,1)}, u32[]{:S(2)}) copy-start(bf16[2,192,4096]{2,1,0:T(8,128)(2,1)} %param.25) | copy-start | bytes 9437188
  145.2 1.3 copy-start.1
  153.4 36.3 %copy-start.7 = (f32[32,8]{0,1:T(8,128)S(1)}, f32[32,8]{0,1:T(8,128)}, u32[]{:S(2)}) copy-start(f32[32,8]{0,1:T(8,128)} %param.24) | copy-start | bytes 3076
  185.1 19.2 %all-to-all-start.2 = ((bf16[4,2,32,1024]{3,2,1,0:T(8,128)(2,1)}), bf16[4,2,32,1024]{3,2,1,0:T(8,128)(2,1)}, u32[]{:S(2)}, u32[]{:S(2)}) async-start(bf16[4,2,32,1024]{3,2,1,0:T(8,128)(2,1)} %copy.39), calls=%async_computation.3 | async-start | bytes 1048576 | tf_op jit(solution)/shard_map/all_to_all | solution.py:129
Sparse Core Ops, SparseCore 0:
  53.6 32.2 all-reduce.1
  153.5 29.5 reduce-scatter.1
where the time goes:
time: 221 us; the launch traced here: 220 us
  waiting for transfers between devices  87.1 us (39%)
  blocking collectives  69.3 us (31%)
  local copies, waits for them, and re-layouts  14 us (6%)
  between operations  13.6 us (6%)
  matrix products  13.1 us (6%)
  other arithmetic  12.9 us (6%)
  starting transfers between devices  10.2 us (5%)
    all_to_all x1, blocking collectives, per_device(): lax.all_to_all(picked.reshape(ep_count, local_experts, capacity, normed.s...  51.9 us
    psum x1, waiting for transfers between devices, per_device(): hidden_full = lax.psum(with_residual, 'tp')  32.4 us
    reduce_scatter x1, waiting for transfers between devices, per_device(): lax.psum_scatter(partial_out.astype(jnp.bfloat16), 'tp', scatter_dimensio...  29.8 us
    all_gather x1, blocking collectives, per_device(): lax.all_gather(attended, 'ep', axis=0, tiled=True)  17.4 us
    all_to_all x1, waiting for transfers between devices, per_device(): lax.all_to_all(reduced.astype(jnp.bfloat16), 'ep', split_axis=0, concat_a...  14.5 us
    all_to_all x1, waiting for transfers between devices, per_device(): lax.all_to_all(partial_all, 'ep', split_axis=0, concat_axis=1, tiled=True)  10.4 us
    dot_general x1, matrix products, per_device(): jnp.einsum('aesf,efd->aesd', activated, down_proj, preferred_element_type...  5.72 us
    all_to_all x1, starting transfers between devices, per_device(): lax.all_to_all(partial_all, 'ep', split_axis=0, concat_axis=1, tiled=True)  5.52 us
  transfers between devices with their start and end apart: 4, of which 4 were waited for; matrix products, arithmetic and copies ran while one was open for 1% of the time, Pallas kernels for 0%

commit v1 on v0

--- a/solution.py
+++ b/solution.py
@@ -1,8 +1,11 @@
+import functools
 import math
 
 import jax
 import jax.numpy as jnp
 from jax import lax
+from jax.experimental import pallas as pl
+from jax.experimental.pallas import tpu as pltpu
 from jax.sharding import PartitionSpec as P
 
 HEAD_DIM = 128
@@ -135,9 +138,355 @@
     return (hidden + mixture).astype(jnp.bfloat16)
 
 
+MESH = pl.DeviceIdType.MESH
+N = 4
+BF = jnp.bfloat16
+F32 = jnp.float32
+
+
+def dot_nt(a, b):
+    return lax.dot_general(a, b, (((1,), (1,)), ((), ())), preferred_element_type=F32)
+
+
+def layer_kernel(
+    len_ref, q_ref, ck_hbm, cv_hbm, nk_ref, nv_ref, wo_hbm, res_ref, gain_ref, routes_ref, gw_ref,
+    g_hbm, u_hbm, d_hbm, out_ref,
+    ck, cv, wo, gw, uw, dw, qs, ao, nk32, nv32, gain32, rgain, att, res_all, w_all,
+    part, c1s, c1r, hg, ga, ua, ss, act, ecs, ecr, p1, p3, xs, xr, zs, zr,
+    load_sem, res_s, res_r, w_s, w_r, a_s, a_f, a_r, c1_s, c1_rs, cz_s, cz_f, cz_r, cx_s, cx_r,
+    cc_s, cc_r, ec_s, ec_r, ex_s, ex_r, ez_s, ez_r,
+):
+    rows, heads = q_ref.shape[0], q_ref.shape[1] // HEAD_DIM
+    slots = ck.shape[1]
+    width = res_ref.shape[1]
+    quarter = width // N
+    half_rows = rows // 2
+    z = lax.axis_index("ep")
+    t = lax.axis_index("tp")
+    core, xpos = lax.rem(t, 2), t // 2
+    t_core = 2 * xpos + (1 - core)
+    t_x = 2 * (1 - xpos) + core
+    t_diag = 2 * (1 - xpos) + (1 - core)
+    order = [
+        z,
+        jnp.where(z == 0, 1, z - 1),
+        jnp.where(z == 0, 2, jnp.where(z == N - 1, 1, z + 1)),
+        jnp.where(z <= 1, 3, 0),
+    ]
+    always = z >= 0
+    sends = []
+
+    def load(i, src, dst):
+        copy = pltpu.make_async_copy(src, dst, load_sem.at[i])
+        copy.start()
+        return copy
+
+    def send(src, dst, s_sem, r_sem, where, cond=None):
+        copy = pltpu.make_async_remote_copy(
+            src_ref=src, dst_ref=dst, send_sem=s_sem, recv_sem=r_sem, device_id=where,
+            device_id_type=MESH,
+        )
+        if cond is None:
+            copy.start()
+        else:
+            pl.when(cond)(lambda: copy.start())
+        sends.append((copy, cond))
+
+    def arrived(dst, s_sem, r_sem):
+        pltpu.make_async_remote_copy(
+            src_ref=dst, dst_ref=dst, send_sem=s_sem, recv_sem=r_sem, device_id={"ep": z},
+            device_id_type=MESH,
+        ).wait_recv()
+
+    loads = []
+    for h in range(2):
+        piece = pl.ds(h * half_rows, half_rows)
+        loads.append(load(2 * h, ck_hbm.at[piece], ck.at[piece]))
+        loads.append(load(2 * h + 1, cv_hbm.at[piece], cv.at[piece]))
+    load_wo = load(4, wo_hbm, wo)
+
+    barrier = pltpu.get_barrier_semaphore()
+    for k in range(1, N):
+        pl.semaphore_signal(barrier, inc=1, device_id={"ep": lax.rem(z + k, N)}, device_id_type=MESH)
+        pl.semaphore_signal(barrier, inc=1, device_id={"tp": lax.rem(t + k, N)}, device_id_type=MESH)
+
+    lane = lax.broadcasted_iota(jnp.int32, (rows, 128), 1)
+    dense = jnp.zeros((rows, 128), F32)
+    for k in range(TOP):
+        dense = dense + jnp.where(lane == routes_ref[:, k : k + 1], gw_ref[:, k : k + 1], 0.0)
+    w_all[z] = dense
+    for h in range(heads):
+        qs[pl.ds(h, rows, stride=heads), :] = q_ref[:, h * HEAD_DIM : (h + 1) * HEAD_DIM].astype(F32)
+    nk32[...] = nk_ref[...].astype(F32)
+    nv32[...] = nv_ref[...].astype(F32)
+    gain32[...] = gain_ref[...].astype(F32)
+    rgain[...] = 1.0 / gain32[...]
+    ga[...] = jnp.zeros_like(ga)
+    ua[...] = jnp.zeros_like(ua)
+    ss[...] = jnp.zeros_like(ss)
+
+    pl.semaphore_wait(barrier, 2 * (N - 1))
+
+    send(res_ref, res_all.at[z], res_s.at[0], res_r.at[z], {"ep": t}, z != t)
+    for k in range(1, N):
+        send(w_all.at[z], w_all.at[z], w_s.at[k], w_r.at[z], {"ep": lax.rem(z + k, N)})
+
+    score_scale = 1.0 / math.sqrt(HEAD_DIM)
+    position = lax.broadcasted_iota(jnp.int32, (heads, slots), 1)
+    group = 8
+    for h in range(2):
+        loads[2 * h].wait()
+        loads[2 * h + 1].wait()
+
+        def some_rows(g, carry):
+            for i in range(group):
+                r = h * half_rows + g * group + i
+                q32 = qs[pl.ds(pl.multiple_of(r * heads, heads), heads), :]
+                scores = dot_nt(q32.astype(BF), ck[r]) * score_scale
+                own = jnp.sum(q32 * nk32[pl.ds(r, 1), :], axis=1, keepdims=True) * score_scale
+                scores = jnp.where(position < len_ref[r], scores, -jnp.inf)
+                highest = jnp.maximum(jnp.max(scores, axis=1, keepdims=True), own)
+                e = jnp.exp(scores - highest)
+                own_e = jnp.exp(own - highest)
+                inv = 1.0 / (jnp.sum(e, axis=1, keepdims=True) + own_e)
+                probs = (e * inv).astype(BF)
+                own_p = (own_e * inv).astype(BF).astype(F32)
+                o = jnp.dot(probs, cv[r], preferred_element_type=F32)
+                o = o + own_p * nv32[pl.ds(r, 1), :]
+                ao[pl.ds(pl.multiple_of(r * heads, heads), heads), :] = o
+            return carry
+
+        lax.fori_loop(0, half_rows // group, some_rows, 0)
+        for j in range(heads):
+            att[z, h * half_rows : (h + 1) * half_rows, j * HEAD_DIM : (j + 1) * HEAD_DIM] = ao[
+                pl.ds(h * half_rows * heads + j, half_rows, stride=heads), :
+            ].astype(BF)
+        piece = att.at[z, pl.ds(h * half_rows, half_rows)]
+        send(piece, piece, a_s.at[0, h], a_r.at[z, h], {"ep": z + 1}, z < N - 1)
+        send(piece, piece, a_s.at[1, h], a_r.at[z, h], {"ep": z - 1}, z > 0)
+        if h == 0:
+            load_g = load(5, g_hbm, gw)
+            load_u = load(6, u_hbm, uw)
+            load_d = load(7, d_hbm, dw)
+    load_wo.wait()
+
+    for i in range(N):
+        s = order[i]
+        if i > 0:
+            onward = jnp.where(s < z, z + 1, z - 1)
+            go = jnp.logical_and(onward >= 0, onward < N)
+            for h in range(2):
+                piece = att.at[s, pl.ds(h * half_rows, half_rows)]
+                arrived(piece, a_f.at[i, h], a_r.at[s, h])
+                send(piece, piece, a_f.at[i, h], a_r.at[s, h], {"ep": onward}, go)
+
+        def project(n, carry):
+            cols = pl.ds(pl.multiple_of(n * quarter, quarter), quarter)
+            part[i, n] = jnp.dot(att[s], wo[:, cols], preferred_element_type=F32)
+            return carry
+
+        lax.fori_loop(0, N, project, 0)
+
+        @pl.when(t == z)
+        def _():
+            if i > 0:
+                arrived(res_all.at[s], res_s.at[0], res_r.at[s])
+                src = res_all.at[s]
+            else:
+                src = res_ref
+            for n in range(N):
+                part[i, n] = part[i, n] + src[:, n * quarter : (n + 1) * quarter].astype(F32)
+
+        c1s[i] = part[i].astype(BF)
+        for k in range(1, N):
+            to = lax.rem(t + k, N)
+            send(c1s.at[i, to], c1r.at[i, k - 1], c1_s.at[i, k], c1_rs.at[i, k], {"tp": to})
+    my_gain = gain32[:, pl.ds(pl.multiple_of(z * width + t * quarter, quarter), quarter)]
+    for i in range(N):
+        s = order[i]
+        total = part[i, t]
+        for k in range(1, N):
+            arrived(c1r.at[i, k - 1], c1_s.at[i, k], c1_rs.at[i, k])
+            total = total + c1r[i, k - 1].astype(F32)
+        hg[z, t, pl.ds(pl.multiple_of(s * rows, rows), rows), :] = (total * my_gain).astype(BF)
+
+    load_g.wait()
+    load_u.wait()
+    for i in range(N):
+        s = order[i]
+        mine = hg.at[s, t]
+        if i == 0:
+            send(mine, mine, cz_s.at[0], cz_r.at[s], {"ep": z + 1}, z < N - 1)
+            send(mine, mine, cz_s.at[1], cz_r.at[s], {"ep": z - 1}, z > 0)
+        else:
+            onward = jnp.where(s < z, z + 1, z - 1)
+            go = jnp.logical_and(onward >= 0, onward < N)
+            arrived(mine, cz_f.at[i], cz_r.at[s])
+            send(mine, mine, cz_f.at[i], cz_r.at[s], {"ep": onward}, go)
+        send(mine, mine, cx_s.at[i], cx_r.at[i], {"tp": t_x})
+        send(mine, mine, cc_s.at[i, 0], cc_r.at[i, 0], {"tp": t_core})
+        for j in ([i - 1] if i > 0 else []) + ([i] if i == N - 1 else []):
+            sj = order[j]
+            theirs = hg.at[sj, t_x]
+            arrived(theirs, cx_s.at[j], cx_r.at[j])
+            send(theirs, theirs, cc_s.at[j, 1], cc_r.at[j, 1], {"tp": t_core})
+            arrived(hg.at[sj, t_core], cc_s.at[j, 0], cc_r.at[j, 0])
+            arrived(hg.at[sj, t_diag], cc_s.at[j, 1], cc_r.at[j, 1])
+
+            def gate_up(b, carry):
+                cols = pl.ds(pl.multiple_of(sj * width + b * quarter, quarter), quarter)
+                block = hg[sj, b]
+                ga[...] += dot_nt(block, gw[:, cols])
+                ua[...] += dot_nt(block, uw[:, cols])
+                plain = block.astype(F32) * rgain[:, cols]
+                square = plain * plain
+                for m in range(quarter // 128):
+                    ss[...] += square[:, m * 128 : (m + 1) * 128]
+                return carry
+
+            lax.fori_loop(0, N, gate_up, 0)
+
+    units = ga.shape[1]
+    per_expert = units // 2
+    for i in range(1, N):
+        s = order[i]
+        arrived(w_all.at[s], w_s.at[i], w_r.at[s])
+    unit = lax.broadcasted_iota(jnp.int32, (rows, units), 1)
+    for s in range(N):
+        at = slice(s * rows, (s + 1) * rows)
+        mean_square = jnp.sum(ss[at], axis=1, keepdims=True) * (1.0 / (N * width))
+        scale = lax.rsqrt(mean_square + 1e-06)
+        dense = w_all[s]
+        w0 = jnp.sum(jnp.where(lane == 2 * z, dense, 0.0), axis=1, keepdims=True)
+        w1 = jnp.sum(jnp.where(lane == 2 * z + 1, dense, 0.0), axis=1, keepdims=True)
+        gate = ga[at] * scale
+        up = ua[at] * scale
+        weight = jnp.where(unit < per_expert, w0, w1)
+        act[at] = (gate / (1.0 + jnp.exp(-gate)) * up * weight).astype(BF)
+
+    load_d.wait()
+    for j, target in enumerate((t_diag, t_x, t_core, t)):
+
+        def down(n, carry):
+            cols = pl.ds(pl.multiple_of(target * width + n * quarter, quarter), quarter)
+            to = pl.ds(pl.multiple_of(n * quarter, quarter), quarter)
+            y = jnp.dot(act[...], dw[:, cols], preferred_element_type=F32)
+            if j == 1:
+                p1[:, to] = y
+            elif j == 3:
+                p3[:, to] = y
+            else:
+                ecs[j // 2, :, to] = y.astype(BF)
+            return carry
+
+        lax.fori_loop(0, N, down, 0)
+        if j % 2 == 0:
+            m = j // 2
+            send(ecs.at[m], ecr.at[m], ec_s.at[m], ec_r.at[m], {"tp": t_core})
+        if j == 1:
+            arrived(ecr.at[0], ec_s.at[0], ec_r.at[0])
+            for i in reversed(range(N)):
+                s = order[i]
+                at = pl.ds(pl.multiple_of(s * rows, rows), rows)
+                xs[i] = (p1[at, :] + ecr[0, at, :].astype(F32)).astype(BF)
+                send(xs.at[i], xr.at[i], ex_s.at[i], ex_r.at[i], {"tp": t_x})
+    arrived(ecr.at[1], ec_s.at[1], ec_r.at[1])
+    for i in reversed(range(N)):
+        s = order[i]
+        at = pl.ds(pl.multiple_of(s * rows, rows), rows)
+        y = p3[at, :] + ecr[1, at, :].astype(F32)
+        arrived(xr.at[i], ex_s.at[i], ex_r.at[i])
+        y = y + xr[i].astype(F32)
+        if i > 0:
+            zs[i] = y.astype(BF)
+            send(zs.at[i], zr.at[z], ez_s.at[i], ez_r.at[z], {"ep": s})
+        else:
+            for b in range(N):
+                cols = pl.ds(pl.multiple_of(t * width + b * quarter, quarter), quarter)
+                p1[:rows, b * quarter : (b + 1) * quarter] = (
+                    y[:, b * quarter : (b + 1) * quarter]
+                    + hg[t, b, pl.ds(pl.multiple_of(z * rows, rows), rows), :].astype(F32)
+                    * rgain[:, cols]
+                )
+    total = p1[:rows, :]
+    for i in range(1, N):
+        s = order[i]
+        arrived(zr.at[s], ez_s.at[i], ez_r.at[s])
+        total = total + zr[s].astype(F32)
+    out_ref[...] = total.astype(out_ref.dtype)
+
+    for copy, cond in sends:
+        if cond is None:
+            copy.wait_send()
+        else:
+            pl.when(cond)(lambda copy=copy: copy.wait_send())
+
+
+def dense_device(
+    queries, cached_key_table, cached_value_table, fresh_token_keys, fresh_token_values, cache_len,
+    out_proj, residual, norm_gain, routes, gate_weights, gate_proj, up_proj, down_proj,
+):
+    rows, heads = queries.shape[0], queries.shape[1] // HEAD_DIM
+    width = residual.shape[1]
+    quarter = width // N
+    units = gate_proj.shape[0] * gate_proj.shape[1]
+    all_width = N * width
+    all_rows = N * rows
+    flat = lambda w: w.reshape(units, all_width)
+    vm, hbm = pl.BlockSpec(memory_space=pltpu.VMEM), pl.BlockSpec(memory_space=pl.ANY)
+    smem = pl.BlockSpec(memory_space=pltpu.SMEM)
+    V = pltpu.VMEM
+    dma = pltpu.SemaphoreType.DMA
+    scratch = [
+        V(cached_key_table.shape, BF), V(cached_value_table.shape, BF), V(out_proj.shape, BF),
+        V((units, all_width), BF), V((units, all_width), BF), V((units, all_width), BF),
+        V((rows * heads, HEAD_DIM), F32), V((rows * heads, HEAD_DIM), F32),
+        V((rows, HEAD_DIM), F32), V((rows, HEAD_DIM), F32),
+        V((1, all_width), F32), V((1, all_width), F32),
+        V((N, rows, heads * HEAD_DIM), BF), V((N, rows, width), BF), V((N, rows, 128), F32),
+        V((N, N, rows, quarter), F32), V((N, N, rows, quarter), BF), V((N, N - 1, rows, quarter), BF),
+        V((N, N, all_rows, quarter), BF), V((all_rows, units), F32), V((all_rows, units), F32),
+        V((all_rows, 128), F32), V((all_rows, units), BF),
+        V((2, all_rows, width), BF), V((2, all_rows, width), BF),
+        V((all_rows, width), F32), V((all_rows, width), F32),
+        V((N, rows, width), BF), V((N, rows, width), BF), V((N, rows, width), BF), V((N, rows, width), BF),
+        dma((8,)), dma((1,)), dma((N,)), dma((N,)), dma((N,)),
+        dma((2, 2)), dma((N, 2)), dma((N, 2)), dma((N, N)), dma((N, N)),
+        dma((2,)), dma((N,)), dma((N,)), dma((N,)), dma((N,)), dma((N, 2)), dma((N, 2)),
+        dma((2,)), dma((2,)), dma((N,)), dma((N,)), dma((N,)), dma((N,)),
+    ]
+    return pl.pallas_call(
+        layer_kernel,
+        out_shape=jax.ShapeDtypeStruct((rows, width), BF),
+        in_specs=[smem, vm, hbm, hbm, vm, vm, hbm, vm, vm, vm, vm, hbm, hbm, hbm],
+        out_specs=vm,
+        scratch_shapes=scratch,
+        compiler_params=pltpu.CompilerParams(
+            collective_id=0, has_side_effects=True, vmem_limit_bytes=48 * 1024 * 1024
+        ),
+        name="layer",
+    )(
+        cache_len, queries, cached_key_table, cached_value_table, fresh_token_keys,
+        fresh_token_values, out_proj, residual, norm_gain.reshape(1, -1), routes, gate_weights,
+        flat(gate_proj), flat(up_proj), flat(down_proj),
+    )
+
+
+def pick_plan(mesh):
+    def plan(*args):
+        expert_count = args[11].shape[0] * mesh.shape["ep"]
+        square = mesh.shape["ep"] == N and mesh.shape["tp"] == N
+        one_kv_head = args[1].shape[2] == HEAD_DIM
+        if square and one_kv_head and expert_count == TOP:
+            return dense_device(*args)
+        return per_device(*args)
+
+    return plan
+
+
 def solution(mesh):
     return jax.shard_map(
-        per_device,
+        pick_plan(mesh),
         mesh=mesh,
         in_specs=(
             P(("groups", "ep"), "tp"),

time: 221 us -> 73.5 us (0.33)
  waiting for transfers between devices: 87.1 us -> 0 us
  blocking collectives: 69.3 us -> 0 us
  Pallas kernels: 0 us -> 62 us
  between operations: 13.6 us -> 0.02 us
  matrix products: 13.1 us -> 0 us
  other arithmetic: 12.9 us -> 0 us
  starting transfers between devices: 10.2 us -> 0 us
  local copies, waits for them, and re-layouts: 14 us -> 11 us
    pallas_call x0 -> x1, Pallas kernels: none -> 62 us  [dense_device(): pl.pallas_call(layer_kernel, out_shape=jax.ShapeDtypeStruct((rows, width)...]
    all_to_all x1 -> x0, blocking collectives: 51.9 us -> none  [per_device(): lax.all_to_all(picked.reshape(ep_count, local_experts, capacity, normed.s...]
    psum x1 -> x0, waiting for transfers between devices: 32.4 us -> none  [per_device(): hidden_full = lax.psum(with_residual, 'tp')]
    reduce_scatter x1 -> x0, waiting for transfers between devices: 29.8 us -> none  [per_device(): lax.psum_scatter(partial_out.astype(jnp.bfloat16), 'tp', scatter_dimensio...]
    all_to_all x2 -> x0, waiting for transfers between devices: 24.9 us -> none  [the longest x1 14.5 us: per_device(): lax.all_to_all(reduced.astype(jnp.bfloat16), 'ep', split_axis=0, concat_a...]
    all_gather x1 -> x0, blocking collectives: 17.4 us -> none  [per_device(): lax.all_gather(attended, 'ep', axis=0, tiled=True)]
    dot_general x6 -> x0, matrix products: 13.1 us -> none  [the longest x1 5.72 us: per_device(): jnp.einsum('aesf,efd->aesd', activated, down_proj, preferred_element_type...]
    all_to_all x2 -> x0, starting transfers between devices: 10.1 us -> none  [the longest x1 5.52 us: per_device(): lax.all_to_all(partial_all, 'ep', split_axis=0, concat_axis=1, tiled=True)]
  transfers between devices with their start and end apart: 4 -> 0, of which waited for: 4 -> 0; matrix products, arithmetic and copies ran while one was open for 1% -> 0% of each run, Pallas kernels for 0% -> 0%
where the time goes in v1:
time: 73.5 us; the launch traced here: 73 us
  Pallas kernels  62 us (84%)
  local copies, waits for them, and re-layouts  11 us (15%)
    pallas_call x1, Pallas kernels, dense_device(): pl.pallas_call(layer_kernel, out_shape=jax.ShapeDtypeStruct((rows, width)...  62 us
    unnamed x19, local copies, waits for them, and re-layouts  10.3 us

profile of v1, /device:TPU:0, one launch (start us, length us, event | category | flops | bytes accessed | tf_op | source)
XLA Modules:
  0.0 73.0 jit_solution(2635300043168375385)
XLA Ops:
  0.0 0.7 reshape.12.gain_ref
  0.7 0.8 %copy.15.routes_ref = s32[32,8]{1,0:T(8,128)S(1)} copy(s32[32,8]{0,1:T(8,128)} %param.23) | data formatting | bytes 2048 | tf_op args[9]
  1.5 0.8 %copy.16.gw_ref = f32[32,8]{1,0:T(8,128)S(1)} copy(f32[32,8]{0,1:T(8,128)} %param.24) | data formatting | bytes 2048 | tf_op args[10]
  2.2 0.0 copy-start
  2.2 1.9 %copy-done = bf16[2,192,4096]{2,1,0:T(8,128)(2,1)S(1)} copy-done((bf16[2,192,4096]{2,1,0:T(8,128)(2,1)S(1)}, bf16[2,192,4096]{2,1,0:T(8,128)(2,1)}, u32[]{:S(2)}) %copy-start) | copy-done | bytes 3145752
  4.1 0.0 copy-start.1
  4.1 1.2 %copy-done.1 = bf16[32,128,128]{2,1,0:T(8,128)(2,1)S(1)} copy-done((bf16[32,128,128]{2,1,0:T(8,128)(2,1)S(1)}, bf16[32,128,128]{2,1,0:T(8,128)(2,1)}, u32[]{:S(2)}) %copy-start.1) | copy-done | bytes 1048600
  5.4 0.0 copy-start.2
  5.4 1.2 %copy-done.2 = bf16[32,128,128]{2,1,0:T(8,128)(2,1)S(1)} copy-done((bf16[32,128,128]{2,1,0:T(8,128)(2,1)S(1)}, bf16[32,128,128]{2,1,0:T(8,128)(2,1)}, u32[]{:S(2)}) %copy-start.2) | copy-done | bytes 1048600
  6.6 0.0 copy-start.3
  6.6 0.9 %copy-done.3 = bf16[32,2048]{1,0:T(8,128)(2,1)S(1)} copy-done((bf16[32,2048]{1,0:T(8,128)(2,1)S(1)}, bf16[32,2048]{1,0:T(8,128)(2,1)}, u32[]{:S(2)}) %copy-start.3) | copy-done | bytes 131096
  7.5 0.0 copy-start.4
  7.5 0.8 %copy-done.4 = bf16[32,1024]{1,0:T(8,128)(2,1)S(1)} copy-done((bf16[32,1024]{1,0:T(8,128)(2,1)S(1)}, bf16[32,1024]{1,0:T(8,128)(2,1)}, u32[]{:S(2)}) %copy-start.4) | copy-done | bytes 65560
  8.3 0.0 copy-start.5
  8.3 0.7 copy-done.5
  9.0 0.0 copy-start.6
  9.0 0.7 copy-done.6
  9.7 0.0 copy-start.7
  9.7 0.7 copy-done.7
  10.4 62.0 %layer.1 = bf16[32,1024]{1,0:T(8,128)(2,1)S(1)} custom-call(s32[32]{0:T(128)S(1)} %copy-done.7, bf16[32,2048]{1,0:T(8,128)(2,1)S(1)} %copy-done.3, bf16[32,128,128]{2,1,0:T(8,128)(2,1)S(1)} %copy-done.1, bf16[32,128,128]{2,1,0:T(8,128)(2,1)S(1)} %copy-done.2, bf16[32,128]{1,0:T(8,128)(2,1)S(1)} %copy-done.5, bf16[32,128]{1,0:T(8,128)(2,1)S(1)} %copy-done.6, ...), custom_call_target="tpu_custom_call" | custom-call | tf_op jit(solution)/shard_map/layer/pallas_call | solution.py:458
  72.4 0.6 copy.18
Async XLA Ops:
  2.2 1.9 %copy-start = (bf16[2,192,4096]{2,1,0:T(8,128)(2,1)S(1)}, bf16[2,192,4096]{2,1,0:T(8,128)(2,1)}, u32[]{:S(2)}) copy-start(bf16[2,192,4096]{2,1,0:T(8,128)(2,1)} %param.25) | copy-start | bytes 9437188
  4.1 1.2 %copy-start.1 = (bf16[32,128,128]{2,1,0:T(8,128)(2,1)S(1)}, bf16[32,128,128]{2,1,0:T(8,128)(2,1)}, u32[]{:S(2)}) copy-start(bf16[32,128,128]{2,1,0:T(8,128)(2,1)} %ck_hbm.1) | copy-start | bytes 3145732
  5.4 1.2 %copy-start.2 = (bf16[32,128,128]{2,1,0:T(8,128)(2,1)S(1)}, bf16[32,128,128]{2,1,0:T(8,128)(2,1)}, u32[]{:S(2)}) copy-start(bf16[32,128,128]{2,1,0:T(8,128)(2,1)} %cv_hbm.1) | copy-start | bytes 3145732
  6.6 0.9 %copy-start.3 = (bf16[32,2048]{1,0:T(8,128)(2,1)S(1)}, bf16[32,2048]{1,0:T(8,128)(2,1)}, u32[]{:S(2)}) copy-start(bf16[32,2048]{1,0:T(8,128)(2,1)} %q_ref.1) | copy-start | bytes 393220
  7.5 0.8 %copy-start.4 = (bf16[32,1024]{1,0:T(8,128)(2,1)S(1)}, bf16[32,1024]{1,0:T(8,128)(2,1)}, u32[]{:S(2)}) copy-start(bf16[32,1024]{1,0:T(8,128)(2,1)} %res_ref.1) | copy-start | bytes 196612
  8.3 0.7 copy-start.5
  9.0 0.7 copy-start.6
  9.7 0.7 copy-start.7

commit v2 on v1

--- a/solution.py
+++ b/solution.py
@@ -1,4 +1,3 @@
-import functools
 import math
 
 import jax
@@ -149,9 +148,9 @@
 
 
 def layer_kernel(
-    len_ref, q_ref, ck_hbm, cv_hbm, nk_ref, nv_ref, wo_hbm, res_ref, gain_ref, routes_ref, gw_ref,
+    len_hbm, q_hbm, ck_hbm, cv_hbm, nk_hbm, nv_hbm, wo_hbm, res_hbm, gain_hbm, routes_hbm, gw_hbm,
     g_hbm, u_hbm, d_hbm, out_ref,
-    ck, cv, wo, gw, uw, dw, qs, ao, nk32, nv32, gain32, rgain, att, res_all, w_all,
+    len_ref, q_ref, nk_ref, nv_ref, res_ref, gain_ref, routes_ref, gw_ref, ck, cv, wo, gw, uw, dw, qs, ao, nk32, nv32, gain32, rgain, att, res_all, w_all,
     part, c1s, c1r, hg, ga, ua, ss, act, ecs, ecr, p1, p3, xs, xr, zs, zr,
     load_sem, res_s, res_r, w_s, w_r, a_s, a_f, a_r, c1_s, c1_rs, cz_s, cz_f, cz_r, cx_s, cx_r,
     cc_s, cc_r, ec_s, ec_r, ex_s, ex_r, ez_s, ez_r,
@@ -198,38 +197,44 @@
             device_id_type=MESH,
         ).wait_recv()
 
+    load_q = load(8, q_hbm, q_ref)
     loads = []
     for h in range(2):
         piece = pl.ds(h * half_rows, half_rows)
         loads.append(load(2 * h, ck_hbm.at[piece], ck.at[piece]))
         loads.append(load(2 * h + 1, cv_hbm.at[piece], cv.at[piece]))
-    load_wo = load(4, wo_hbm, wo)
+    pairs = (
+        (len_hbm, len_ref), (nk_hbm, nk_ref), (nv_hbm, nv_ref), (res_hbm, res_ref),
+        (gain_hbm, gain_ref), (routes_hbm, routes_ref), (gw_hbm, gw_ref),
+    )
+    small = [load(9 + i, src, dst) for i, (src, dst) in enumerate(pairs)]
 
     barrier = pltpu.get_barrier_semaphore()
     for k in range(1, N):
         pl.semaphore_signal(barrier, inc=1, device_id={"ep": lax.rem(z + k, N)}, device_id_type=MESH)
         pl.semaphore_signal(barrier, inc=1, device_id={"tp": lax.rem(t + k, N)}, device_id_type=MESH)
 
+    ga[...] = jnp.zeros_like(ga)
+    ua[...] = jnp.zeros_like(ua)
+    ss[...] = jnp.zeros_like(ss)
+    for copy in small:
+        copy.wait()
     lane = lax.broadcasted_iota(jnp.int32, (rows, 128), 1)
+    routes = jnp.transpose(routes_ref[...])
+    weights = jnp.transpose(gw_ref[...])
     dense = jnp.zeros((rows, 128), F32)
     for k in range(TOP):
-        dense = dense + jnp.where(lane == routes_ref[:, k : k + 1], gw_ref[:, k : k + 1], 0.0)
+        dense = dense + jnp.where(lane == routes[:, k : k + 1], weights[:, k : k + 1], 0.0)
     w_all[z] = dense
+    load_q.wait()
     for h in range(heads):
         qs[pl.ds(h, rows, stride=heads), :] = q_ref[:, h * HEAD_DIM : (h + 1) * HEAD_DIM].astype(F32)
     nk32[...] = nk_ref[...].astype(F32)
     nv32[...] = nv_ref[...].astype(F32)
-    gain32[...] = gain_ref[...].astype(F32)
+    gain = gain_ref[...].astype(F32)
+    for j in range(gain.shape[0]):
+        gain32[:, j * 128 : (j + 1) * 128] = gain[j : j + 1, :]
     rgain[...] = 1.0 / gain32[...]
-    ga[...] = jnp.zeros_like(ga)
-    ua[...] = jnp.zeros_like(ua)
-    ss[...] = jnp.zeros_like(ss)
-
-    pl.semaphore_wait(barrier, 2 * (N - 1))
-
-    send(res_ref, res_all.at[z], res_s.at[0], res_r.at[z], {"ep": t}, z != t)
-    for k in range(1, N):
-        send(w_all.at[z], w_all.at[z], w_s.at[k], w_r.at[z], {"ep": lax.rem(z + k, N)})
 
     score_scale = 1.0 / math.sqrt(HEAD_DIM)
     position = lax.broadcasted_iota(jnp.int32, (heads, slots), 1)
@@ -237,23 +242,34 @@
     for h in range(2):
         loads[2 * h].wait()
         loads[2 * h + 1].wait()
+        if h == 0:
+            load_wo = load(4, wo_hbm, wo)
 
         def some_rows(g, carry):
+            first = h * half_rows + g * group
+            at = pl.ds(pl.multiple_of(first * heads, group * heads), group * heads)
+            q32 = qs[at, :]
+            q16 = q32.astype(BF)
+            scores, fresh_k, fresh_v = [], [], []
             for i in range(group):
-                r = h * half_rows + g * group + i
-                q32 = qs[pl.ds(pl.multiple_of(r * heads, heads), heads), :]
-                scores = dot_nt(q32.astype(BF), ck[r]) * score_scale
-                own = jnp.sum(q32 * nk32[pl.ds(r, 1), :], axis=1, keepdims=True) * score_scale
-                scores = jnp.where(position < len_ref[r], scores, -jnp.inf)
-                highest = jnp.maximum(jnp.max(scores, axis=1, keepdims=True), own)
-                e = jnp.exp(scores - highest)
-                own_e = jnp.exp(own - highest)
-                inv = 1.0 / (jnp.sum(e, axis=1, keepdims=True) + own_e)
-                probs = (e * inv).astype(BF)
-                own_p = (own_e * inv).astype(BF).astype(F32)
-                o = jnp.dot(probs, cv[r], preferred_element_type=F32)
-                o = o + own_p * nv32[pl.ds(r, 1), :]
-                ao[pl.ds(pl.multiple_of(r * heads, heads), heads), :] = o
+                one = q16[i * heads : (i + 1) * heads]
+                dots = dot_nt(one, ck[first + i]) * score_scale
+                scores.append(jnp.where(position < len_ref[first + i], dots, -jnp.inf))
+                fresh_k.append(jnp.broadcast_to(nk32[pl.ds(first + i, 1), :], (heads, HEAD_DIM)))
+                fresh_v.append(jnp.broadcast_to(nv32[pl.ds(first + i, 1), :], (heads, HEAD_DIM)))
+            scores = jnp.concatenate(scores, axis=0)
+            own = jnp.sum(q32 * jnp.concatenate(fresh_k, axis=0), axis=1, keepdims=True) * score_scale
+            highest = jnp.maximum(jnp.max(scores, axis=1, keepdims=True), own)
+            e = jnp.exp(scores - highest)
+            own_e = jnp.exp(own - highest)
+            inv = 1.0 / (jnp.sum(e, axis=1, keepdims=True) + own_e)
+            probs = (e * inv).astype(BF)
+            own_p = (own_e * inv).astype(BF).astype(F32)
+            o = [
+                jnp.dot(probs[i * heads : (i + 1) * heads], cv[first + i], preferred_element_type=F32)
+                for i in range(group)
+            ]
+            ao[at, :] = jnp.concatenate(o, axis=0) + own_p * jnp.concatenate(fresh_v, axis=0)
             return carry
 
         lax.fori_loop(0, half_rows // group, some_rows, 0)
@@ -261,6 +277,8 @@
             att[z, h * half_rows : (h + 1) * half_rows, j * HEAD_DIM : (j + 1) * HEAD_DIM] = ao[
                 pl.ds(h * half_rows * heads + j, half_rows, stride=heads), :
             ].astype(BF)
+        if h == 0:
+            pl.semaphore_wait(barrier, 2 * (N - 1))
         piece = att.at[z, pl.ds(h * half_rows, half_rows)]
         send(piece, piece, a_s.at[0, h], a_r.at[z, h], {"ep": z + 1}, z < N - 1)
         send(piece, piece, a_s.at[1, h], a_r.at[z, h], {"ep": z - 1}, z > 0)
@@ -268,6 +286,9 @@
             load_g = load(5, g_hbm, gw)
             load_u = load(6, u_hbm, uw)
             load_d = load(7, d_hbm, dw)
+            send(res_ref, res_all.at[z], res_s.at[0], res_r.at[z], {"ep": t}, z != t)
+            for k in range(1, N):
+                send(w_all.at[z], w_all.at[z], w_s.at[k], w_r.at[z], {"ep": lax.rem(z + k, N)})
     load_wo.wait()
 
     for i in range(N):
@@ -433,11 +454,14 @@
     all_width = N * width
     all_rows = N * rows
     flat = lambda w: w.reshape(units, all_width)
-    vm, hbm = pl.BlockSpec(memory_space=pltpu.VMEM), pl.BlockSpec(memory_space=pl.ANY)
-    smem = pl.BlockSpec(memory_space=pltpu.SMEM)
+    vm, hbm = pl.BlockSpec(memory_space=pltpu.VMEM), pl.BlockSpec(memory_space=pltpu.HBM)
     V = pltpu.VMEM
     dma = pltpu.SemaphoreType.DMA
+    gain = norm_gain.reshape(-1, 128)
     scratch = [
+        pltpu.SMEM(cache_len.shape, jnp.int32), V(queries.shape, BF),
+        V(fresh_token_keys.shape, BF), V(fresh_token_values.shape, BF), V(residual.shape, BF),
+        V(gain.shape, BF), V((TOP, rows), jnp.int32), V((TOP, rows), F32),
         V(cached_key_table.shape, BF), V(cached_value_table.shape, BF), V(out_proj.shape, BF),
         V((units, all_width), BF), V((units, all_width), BF), V((units, all_width), BF),
         V((rows * heads, HEAD_DIM), F32), V((rows * heads, HEAD_DIM), F32),
@@ -450,7 +474,7 @@
         V((2, all_rows, width), BF), V((2, all_rows, width), BF),
         V((all_rows, width), F32), V((all_rows, width), F32),
         V((N, rows, width), BF), V((N, rows, width), BF), V((N, rows, width), BF), V((N, rows, width), BF),
-        dma((8,)), dma((1,)), dma((N,)), dma((N,)), dma((N,)),
+        dma((16,)), dma((1,)), dma((N,)), dma((N,)), dma((N,)),
         dma((2, 2)), dma((N, 2)), dma((N, 2)), dma((N, N)), dma((N, N)),
         dma((2,)), dma((N,)), dma((N,)), dma((N,)), dma((N,)), dma((N, 2)), dma((N, 2)),
         dma((2,)), dma((2,)), dma((N,)), dma((N,)), dma((N,)), dma((N,)),
@@ -458,16 +482,16 @@
     return pl.pallas_call(
         layer_kernel,
         out_shape=jax.ShapeDtypeStruct((rows, width), BF),
-        in_specs=[smem, vm, hbm, hbm, vm, vm, hbm, vm, vm, vm, vm, hbm, hbm, hbm],
+        in_specs=[hbm] * 14,
         out_specs=vm,
         scratch_shapes=scratch,
         compiler_params=pltpu.CompilerParams(
-            collective_id=0, has_side_effects=True, vmem_limit_bytes=48 * 1024 * 1024
+            collective_id=0, has_side_effects=True, vmem_limit_bytes=63 * 1024 * 1024
         ),
         name="layer",
     )(
         cache_len, queries, cached_key_table, cached_value_table, fresh_token_keys,
-        fresh_token_values, out_proj, residual, norm_gain.reshape(1, -1), routes, gate_weights,
+        fresh_token_values, out_proj, residual, gain, routes.T, gate_weights.T,
         flat(gate_proj), flat(up_proj), flat(down_proj),
     )
 

time: 73.5 us -> 58.7 us (0.80)
  local copies, waits for them, and re-layouts: 11 us -> 1.47 us
  Pallas kernels: 62 us -> 57.1 us
    unnamed x19 -> x1, local copies, waits for them, and re-layouts: 10.3 us -> 1.47 us
    pallas_call x1, Pallas kernels: 62 us -> 57.1 us  [dense_device(): pl.pallas_call(layer_kernel, out_shape=jax.ShapeDtypeStruct((rows, width)...]
where the time goes in v2:
time: 58.7 us; the launch traced here: 58.5 us
  Pallas kernels  57.1 us (97%)
  local copies, waits for them, and re-layouts  1.47 us (3%)
    pallas_call x1, Pallas kernels, dense_device(): pl.pallas_call(layer_kernel, out_shape=jax.ShapeDtypeStruct((rows, width)...  57.1 us
    unnamed x1, local copies, waits for them, and re-layouts  1.47 us

profile of v2, /device:TPU:0, one launch (start us, length us, event | category | flops | bytes accessed | tf_op | source)
XLA Modules:
  0.0 58.5 jit_solution(12944758226141425581)
XLA Ops:
  0.0 57.1 %layer.1 = bf16[32,1024]{1,0:T(8,128)(2,1)} custom-call(s32[32]{0:T(128)} %len_hbm.1, bf16[32,2048]{1,0:T(8,128)(2,1)} %q_hbm.1, bf16[32,128,128]{2,1,0:T(8,128)(2,1)} %ck_hbm.1, bf16[32,128,128]{2,1,0:T(8,128)(2,1)} %cv_hbm.1, bf16[32,128]{1,0:T(8,128)(2,1)} %nk_hbm.1, bf16[32,128]{1,0:T(8,128)(2,1)} %nv_hbm.1, bf16[2048,1024]{1,0:T(8,128)(2,1)} %wo_hbm.1, ...), custom_call_target="tpu_custom_call" | custom-call | tf_op jit(solution)/shard_map/layer/pallas_call | solution.py:482
  57.1 1.5 %copy.16 = bf16[32,1024]{1,0:T(8,128)(2,1)} copy(bf16[32,1024]{1,0:T(8,128)(2,1)} %layer.1) | data formatting | bytes 131072

commit v3 on v2

--- a/solution.py
+++ b/solution.py
@@ -151,8 +151,8 @@
     len_hbm, q_hbm, ck_hbm, cv_hbm, nk_hbm, nv_hbm, wo_hbm, res_hbm, gain_hbm, routes_hbm, gw_hbm,
     g_hbm, u_hbm, d_hbm, out_ref,
     len_ref, q_ref, nk_ref, nv_ref, res_ref, gain_ref, routes_ref, gw_ref, ck, cv, wo, gw, uw, dw, qs, ao, nk32, nv32, gain32, rgain, att, res_all, w_all,
-    part, c1s, c1r, hg, ga, ua, ss, act, ecs, ecr, p1, p3, xs, xr, zs, zr,
-    load_sem, res_s, res_r, w_s, w_r, a_s, a_f, a_r, c1_s, c1_rs, cz_s, cz_f, cz_r, cx_s, cx_r,
+    part, c1s, c1r, hg, ga, ua, ss, act, ecs, ecr, p1, p3, xs, xr, zs, zr, wsum,
+    load_sem, res_s, res_r, w_s, w_r, a_s, a_f, a_r, c1_s, c1_rs, cz_s, cz_r, cx_s, cx_r,
     cc_s, cc_r, ec_s, ec_r, ex_s, ex_r, ez_s, ez_r,
 ):
     rows, heads = q_ref.shape[0], q_ref.shape[1] // HEAD_DIM
@@ -219,12 +219,12 @@
     ss[...] = jnp.zeros_like(ss)
     for copy in small:
         copy.wait()
-    lane = lax.broadcasted_iota(jnp.int32, (rows, 128), 1)
-    routes = jnp.transpose(routes_ref[...])
-    weights = jnp.transpose(gw_ref[...])
-    dense = jnp.zeros((rows, 128), F32)
+    expert = lax.broadcasted_iota(jnp.int32, (TOP, rows), 0)
+    dense = jnp.zeros((TOP, rows), F32)
     for k in range(TOP):
-        dense = dense + jnp.where(lane == routes[:, k : k + 1], weights[:, k : k + 1], 0.0)
+        dense = dense + jnp.where(expert == routes_ref[k : k + 1, :], gw_ref[k : k + 1, :], 0.0)
+    owner = lax.broadcasted_iota(jnp.int32, (TOP, N * rows), 1) // rows
+    dense = jnp.where(owner == z, jnp.concatenate([dense] * N, axis=1), 0.0)
     w_all[z] = dense
     load_q.wait()
     for h in range(heads):
@@ -237,8 +237,10 @@
     rgain[...] = 1.0 / gain32[...]
 
     score_scale = 1.0 / math.sqrt(HEAD_DIM)
-    position = lax.broadcasted_iota(jnp.int32, (heads, slots), 1)
     group = 8
+    position = lax.broadcasted_iota(jnp.int32, (slots, group * heads), 0)
+    lane_row = lax.broadcasted_iota(jnp.int32, (1, group * heads), 1) // heads
+    own_block = lax.broadcasted_iota(jnp.int32, (group, group * heads), 0) == lane_row
     for h in range(2):
         loads[2 * h].wait()
         loads[2 * h + 1].wait()
@@ -248,28 +250,33 @@
         def some_rows(g, carry):
             first = h * half_rows + g * group
             at = pl.ds(pl.multiple_of(first * heads, group * heads), group * heads)
-            q32 = qs[at, :]
-            q16 = q32.astype(BF)
-            scores, fresh_k, fresh_v = [], [], []
+            q16 = qs[at, :].astype(BF)
+            fresh_k = nk32[pl.ds(pl.multiple_of(first, group), group), :].astype(BF)
+            fresh_v = nv32[pl.ds(pl.multiple_of(first, group), group), :]
+            scores = jnp.zeros((slots, group * heads), F32)
+            lengths = jnp.zeros((1, group * heads), jnp.int32)
             for i in range(group):
-                one = q16[i * heads : (i + 1) * heads]
-                dots = dot_nt(one, ck[first + i]) * score_scale
-                scores.append(jnp.where(position < len_ref[first + i], dots, -jnp.inf))
-                fresh_k.append(jnp.broadcast_to(nk32[pl.ds(first + i, 1), :], (heads, HEAD_DIM)))
-                fresh_v.append(jnp.broadcast_to(nv32[pl.ds(first + i, 1), :], (heads, HEAD_DIM)))
-            scores = jnp.concatenate(scores, axis=0)
-            own = jnp.sum(q32 * jnp.concatenate(fresh_k, axis=0), axis=1, keepdims=True) * score_scale
-            highest = jnp.maximum(jnp.max(scores, axis=1, keepdims=True), own)
+                own_lanes = lane_row == i
+                scores = jnp.where(own_lanes, dot_nt(ck[first + i], q16), scores)
+                lengths = jnp.where(own_lanes, len_ref[first + i], lengths)
+            scores = jnp.where(position < lengths, scores * score_scale, -jnp.inf)
+            own = jnp.sum(jnp.where(own_block, dot_nt(fresh_k, q16), 0.0), axis=0, keepdims=True)
+            own = own * score_scale
+            highest = jnp.maximum(jnp.max(scores, axis=0, keepdims=True), own)
             e = jnp.exp(scores - highest)
             own_e = jnp.exp(own - highest)
-            inv = 1.0 / (jnp.sum(e, axis=1, keepdims=True) + own_e)
-            probs = (e * inv).astype(BF)
+            inv = 1.0 / (jnp.sum(e, axis=0, keepdims=True) + own_e)
+            probs = jnp.transpose(e * inv).astype(BF)
             own_p = (own_e * inv).astype(BF).astype(F32)
-            o = [
-                jnp.dot(probs[i * heads : (i + 1) * heads], cv[first + i], preferred_element_type=F32)
-                for i in range(group)
-            ]
-            ao[at, :] = jnp.concatenate(o, axis=0) + own_p * jnp.concatenate(fresh_v, axis=0)
+            own_p = jnp.sum(
+                jnp.transpose(jnp.where(own_block, own_p, 0.0)), axis=1, keepdims=True
+            )
+            o = []
+            for i in range(group):
+                rows_i = slice(i * heads, (i + 1) * heads)
+                old = jnp.dot(probs[rows_i], cv[first + i], preferred_element_type=F32)
+                o.append(old + own_p[rows_i] * fresh_v[i : i + 1])
+            ao[at, :] = jnp.concatenate(o, axis=0)
             return carry
 
         lax.fori_loop(0, half_rows // group, some_rows, 0)
@@ -291,7 +298,14 @@
                 send(w_all.at[z], w_all.at[z], w_s.at[k], w_r.at[z], {"ep": lax.rem(z + k, N)})
     load_wo.wait()
 
-    for i in range(N):
+    my_gain = gain32[:, pl.ds(pl.multiple_of(z * width + t * quarter, quarter), quarter)]
+
+    def piece_of(block, zb, p):
+        if p == 0:
+            return block.at[pl.ds(pl.multiple_of(jnp.where(zb <= 1, 0, rows), rows), 3 * rows)]
+        return block.at[pl.ds(pl.multiple_of(jnp.where(zb <= 1, 3 * rows, 0), rows), rows)]
+
+    def project_rows(i):
         s = order[i]
         if i > 0:
             onward = jnp.where(s < z, z + 1, z - 1)
@@ -322,8 +336,8 @@
         for k in range(1, N):
             to = lax.rem(t + k, N)
             send(c1s.at[i, to], c1r.at[i, k - 1], c1_s.at[i, k], c1_rs.at[i, k], {"tp": to})
-    my_gain = gain32[:, pl.ds(pl.multiple_of(z * width + t * quarter, quarter), quarter)]
-    for i in range(N):
+
+    def sum_rows(i):
         s = order[i]
         total = part[i, t]
         for k in range(1, N):
@@ -331,59 +345,91 @@
             total = total + c1r[i, k - 1].astype(F32)
         hg[z, t, pl.ds(pl.multiple_of(s * rows, rows), rows), :] = (total * my_gain).astype(BF)
 
+    def own_side(d, p):
+        s = order[d]
+        mine = piece_of(hg.at[s, t], s, p)
+        if d > 0:
+            arrived(mine, cz_s.at[d, p], cz_r.at[s, p])
+        send(mine, mine, cx_s.at[d, p], cx_r.at[d, p], {"tp": t_x})
+        if d == 0:
+            for k in reversed(range(1, N)):
+                send(mine, mine, cz_s.at[k, p], cz_r.at[z, p], {"ep": order[k]})
+        send(mine, mine, cc_s.at[d, p], cc_r.at[d, p], {"tp": t_core})
+
+    def other_side(d, p):
+        s = order[d]
+        theirs = piece_of(hg.at[s, t_x], s, p)
+        arrived(theirs, cx_s.at[d, p], cx_r.at[d, p])
+        send(theirs, theirs, cc_s.at[N + d, p], cc_r.at[N + d, p], {"tp": t_core})
+
+    def gate_up_of(d):
+        s = order[d]
+        for p in range(2):
+            arrived(piece_of(hg.at[s, t_core], s, p), cc_s.at[d, p], cc_r.at[d, p])
+            arrived(piece_of(hg.at[s, t_diag], s, p), cc_s.at[N + d, p], cc_r.at[N + d, p])
+
+        def gate_up(b, carry):
+            cols = pl.ds(pl.multiple_of(s * width + b * quarter, quarter), quarter)
+            block = hg[s, b]
+            ga[...] += dot_nt(gw[:, cols], block)
+            ua[...] += dot_nt(uw[:, cols], block)
+            plain = block.astype(F32) * rgain[:, cols]
+            square = plain * plain
+            for m in range(quarter // 128):
+                ss[...] += square[:, m * 128 : (m + 1) * 128]
+            return carry
+
+        lax.fori_loop(0, N, gate_up, 0)
+
+    project_rows(0)
+    project_rows(1)
+    sum_rows(0)
+    project_rows(2)
+    sum_rows(1)
+    sum_rows(2)
+    own_side(0, 0)
+    project_rows(3)
+    own_side(1, 0)
+    sum_rows(3)
+    own_side(0, 1)
+    other_side(0, 0)
+    own_side(2, 0)
+    other_side(1, 0)
+    own_side(3, 0)
+    other_side(0, 1)
     load_g.wait()
     load_u.wait()
-    for i in range(N):
-        s = order[i]
-        mine = hg.at[s, t]
-        if i == 0:
-            send(mine, mine, cz_s.at[0], cz_r.at[s], {"ep": z + 1}, z < N - 1)
-            send(mine, mine, cz_s.at[1], cz_r.at[s], {"ep": z - 1}, z > 0)
-        else:
-            onward = jnp.where(s < z, z + 1, z - 1)
-            go = jnp.logical_and(onward >= 0, onward < N)
-            arrived(mine, cz_f.at[i], cz_r.at[s])
-            send(mine, mine, cz_f.at[i], cz_r.at[s], {"ep": onward}, go)
-        send(mine, mine, cx_s.at[i], cx_r.at[i], {"tp": t_x})
-        send(mine, mine, cc_s.at[i, 0], cc_r.at[i, 0], {"tp": t_core})
-        for j in ([i - 1] if i > 0 else []) + ([i] if i == N - 1 else []):
-            sj = order[j]
-            theirs = hg.at[sj, t_x]
-            arrived(theirs, cx_s.at[j], cx_r.at[j])
-            send(theirs, theirs, cc_s.at[j, 1], cc_r.at[j, 1], {"tp": t_core})
-            arrived(hg.at[sj, t_core], cc_s.at[j, 0], cc_r.at[j, 0])
-            arrived(hg.at[sj, t_diag], cc_s.at[j, 1], cc_r.at[j, 1])
-
-            def gate_up(b, carry):
-                cols = pl.ds(pl.multiple_of(sj * width + b * quarter, quarter), quarter)
-                block = hg[sj, b]
-                ga[...] += dot_nt(block, gw[:, cols])
-                ua[...] += dot_nt(block, uw[:, cols])
-                plain = block.astype(F32) * rgain[:, cols]
-                square = plain * plain
-                for m in range(quarter // 128):
-                    ss[...] += square[:, m * 128 : (m + 1) * 128]
-                return carry
-
-            lax.fori_loop(0, N, gate_up, 0)
-
-    units = ga.shape[1]
+    own_side(1, 1)
+    other_side(2, 0)
+    own_side(2, 1)
+    own_side(3, 1)
+    gate_up_of(0)
+    other_side(3, 0)
+    other_side(1, 1)
+    gate_up_of(1)
+    other_side(2, 1)
+    other_side(3, 1)
+    gate_up_of(2)
+    gate_up_of(3)
+
+    units = ga.shape[0]
     per_expert = units // 2
+    dense = w_all[z]
     for i in range(1, N):
         s = order[i]
         arrived(w_all.at[s], w_s.at[i], w_r.at[s])
-    unit = lax.broadcasted_iota(jnp.int32, (rows, units), 1)
-    for s in range(N):
-        at = slice(s * rows, (s + 1) * rows)
-        mean_square = jnp.sum(ss[at], axis=1, keepdims=True) * (1.0 / (N * width))
-        scale = lax.rsqrt(mean_square + 1e-06)
-        dense = w_all[s]
-        w0 = jnp.sum(jnp.where(lane == 2 * z, dense, 0.0), axis=1, keepdims=True)
-        w1 = jnp.sum(jnp.where(lane == 2 * z + 1, dense, 0.0), axis=1, keepdims=True)
+        dense = dense + w_all[s]
+    wsum[...] = dense
+    mean_square = jnp.sum(jnp.transpose(ss[...]), axis=0, keepdims=True) * (1.0 / (N * width))
+    scale = lax.rsqrt(mean_square + 1e-06)
+    for m in range(2):
+        at = slice(m * per_expert, (m + 1) * per_expert)
         gate = ga[at] * scale
-        up = ua[at] * scale
-        weight = jnp.where(unit < per_expert, w0, w1)
-        act[at] = (gate / (1.0 + jnp.exp(-gate)) * up * weight).astype(BF)
+        up = ua[at] * (scale * wsum[pl.ds(2 * z + m, 1), :])
+        ga[at] = gate / (1.0 + jnp.exp(-gate)) * up
+    for m in range(units // 128):
+        at = slice(m * 128, (m + 1) * 128)
+        act[:, at] = jnp.transpose(ga[at]).astype(BF)
 
     load_d.wait()
     for j, target in enumerate((t_diag, t_x, t_core, t)):
@@ -467,16 +513,17 @@
         V((rows * heads, HEAD_DIM), F32), V((rows * heads, HEAD_DIM), F32),
         V((rows, HEAD_DIM), F32), V((rows, HEAD_DIM), F32),
         V((1, all_width), F32), V((1, all_width), F32),
-        V((N, rows, heads * HEAD_DIM), BF), V((N, rows, width), BF), V((N, rows, 128), F32),
+        V((N, rows, heads * HEAD_DIM), BF), V((N, rows, width), BF), V((N, TOP, all_rows), F32),
         V((N, N, rows, quarter), F32), V((N, N, rows, quarter), BF), V((N, N - 1, rows, quarter), BF),
-        V((N, N, all_rows, quarter), BF), V((all_rows, units), F32), V((all_rows, units), F32),
+        V((N, N, all_rows, quarter), BF), V((units, all_rows), F32), V((units, all_rows), F32),
         V((all_rows, 128), F32), V((all_rows, units), BF),
         V((2, all_rows, width), BF), V((2, all_rows, width), BF),
         V((all_rows, width), F32), V((all_rows, width), F32),
         V((N, rows, width), BF), V((N, rows, width), BF), V((N, rows, width), BF), V((N, rows, width), BF),
+        V((TOP, all_rows), F32),
         dma((16,)), dma((1,)), dma((N,)), dma((N,)), dma((N,)),
         dma((2, 2)), dma((N, 2)), dma((N, 2)), dma((N, N)), dma((N, N)),
-        dma((2,)), dma((N,)), dma((N,)), dma((N,)), dma((N,)), dma((N, 2)), dma((N, 2)),
+        dma((N, 2)), dma((N, 2)), dma((N, 2)), dma((N, 2)), dma((2 * N, 2)), dma((2 * N, 2)),
         dma((2,)), dma((2,)), dma((N,)), dma((N,)), dma((N,)), dma((N,)),
     ]
     return pl.pallas_call(

time: 58.7 us -> 56.5 us (0.963)
  Pallas kernels: 57.1 us -> 54.8 us
    pallas_call x1, Pallas kernels: 57.1 us -> 54.8 us  [dense_device(): pl.pallas_call(layer_kernel, out_shape=jax.ShapeDtypeStruct((rows, width)...]
where the time goes in v3:
time: 56.5 us; the launch traced here: 56.3 us
  Pallas kernels  54.8 us (97%)
  local copies, waits for them, and re-layouts  1.47 us (3%)
    pallas_call x1, Pallas kernels, dense_device(): pl.pallas_call(layer_kernel, out_shape=jax.ShapeDtypeStruct((rows, width)...  54.8 us
    unnamed x1, local copies, waits for them, and re-layouts  1.47 us

profile of v3, /device:TPU:0, one launch (start us, length us, event | category | flops | bytes accessed | tf_op | source)
XLA Modules:
  0.0 56.3 jit_solution(16202017611975901086)
XLA Ops:
  0.0 54.8 %layer.1 = bf16[32,1024]{1,0:T(8,128)(2,1)} custom-call(s32[32]{0:T(128)} %len_hbm.1, bf16[32,2048]{1,0:T(8,128)(2,1)} %q_hbm.1, bf16[32,128,128]{2,1,0:T(8,128)(2,1)} %ck_hbm.1, bf16[32,128,128]{2,1,0:T(8,128)(2,1)} %cv_hbm.1, bf16[32,128]{1,0:T(8,128)(2,1)} %nk_hbm.1, bf16[32,128]{1,0:T(8,128)(2,1)} %nv_hbm.1, bf16[2048,1024]{1,0:T(8,128)(2,1)} %wo_hbm.1, ...), custom_call_target="tpu_custom_call" | custom-call | tf_op jit(solution)/shard_map/layer/pallas_call | solution.py:529
  54.8 1.5 %copy.16 = bf16[32,1024]{1,0:T(8,128)(2,1)} copy(bf16[32,1024]{1,0:T(8,128)(2,1)} %layer.1) | data formatting | bytes 131072

commit v4 on v3

--- a/solution.py
+++ b/solution.py
@@ -305,7 +305,7 @@
             return block.at[pl.ds(pl.multiple_of(jnp.where(zb <= 1, 0, rows), rows), 3 * rows)]
         return block.at[pl.ds(pl.multiple_of(jnp.where(zb <= 1, 3 * rows, 0), rows), rows)]
 
-    def project_rows(i):
+    def fetch(i):
         s = order[i]
         if i > 0:
             onward = jnp.where(s < z, z + 1, z - 1)
@@ -314,6 +314,9 @@
                 piece = att.at[s, pl.ds(h * half_rows, half_rows)]
                 arrived(piece, a_f.at[i, h], a_r.at[s, h])
                 send(piece, piece, a_f.at[i, h], a_r.at[s, h], {"ep": onward}, go)
+
+    def project_rows(i):
+        s = order[i]
 
         def project(n, carry):
             cols = pl.ds(pl.multiple_of(n * quarter, quarter), quarter)
@@ -382,10 +385,13 @@
         lax.fori_loop(0, N, gate_up, 0)
 
     project_rows(0)
+    fetch(1)
     project_rows(1)
     sum_rows(0)
+    fetch(2)
     project_rows(2)
     sum_rows(1)
+    fetch(3)
     sum_rows(2)
     own_side(0, 0)
     project_rows(3)
@@ -449,18 +455,23 @@
         lax.fori_loop(0, N, down, 0)
         if j % 2 == 0:
             m = j // 2
-            send(ecs.at[m], ecr.at[m], ec_s.at[m], ec_r.at[m], {"tp": t_core})
+            for i in reversed(range(N)):
+                some = pl.ds(pl.multiple_of(order[i] * rows, rows), rows)
+                send(
+                    ecs.at[m, some], ecr.at[m, some], ec_s.at[m, i], ec_r.at[m, i], {"tp": t_core}
+                )
         if j == 1:
-            arrived(ecr.at[0], ec_s.at[0], ec_r.at[0])
             for i in reversed(range(N)):
                 s = order[i]
+                some = pl.ds(pl.multiple_of(s * rows, rows), rows)
+                arrived(ecr.at[0, some], ec_s.at[0, i], ec_r.at[0, i])
                 at = pl.ds(pl.multiple_of(s * rows, rows), rows)
                 xs[i] = (p1[at, :] + ecr[0, at, :].astype(F32)).astype(BF)
                 send(xs.at[i], xr.at[i], ex_s.at[i], ex_r.at[i], {"tp": t_x})
-    arrived(ecr.at[1], ec_s.at[1], ec_r.at[1])
     for i in reversed(range(N)):
         s = order[i]
         at = pl.ds(pl.multiple_of(s * rows, rows), rows)
+        arrived(ecr.at[1, at], ec_s.at[1, i], ec_r.at[1, i])
         y = p3[at, :] + ecr[1, at, :].astype(F32)
         arrived(xr.at[i], ex_s.at[i], ex_r.at[i])
         y = y + xr[i].astype(F32)
@@ -524,7 +535,7 @@
         dma((16,)), dma((1,)), dma((N,)), dma((N,)), dma((N,)),
         dma((2, 2)), dma((N, 2)), dma((N, 2)), dma((N, N)), dma((N, N)),
         dma((N, 2)), dma((N, 2)), dma((N, 2)), dma((N, 2)), dma((2 * N, 2)), dma((2 * N, 2)),
-        dma((2,)), dma((2,)), dma((N,)), dma((N,)), dma((N,)), dma((N,)),
+        dma((2, N)), dma((2, N)), dma((N,)), dma((N,)), dma((N,)), dma((N,)),
     ]
     return pl.pallas_call(
         layer_kernel,

time: 56.5 us -> 54.6 us (0.966)
  Pallas kernels: 54.8 us -> 52.9 us
    pallas_call x1, Pallas kernels: 54.8 us -> 52.9 us  [dense_device(): pl.pallas_call(layer_kernel, out_shape=jax.ShapeDtypeStruct((rows, width)...]
where the time goes in v4:
time: 54.6 us; the launch traced here: 54.4 us
  Pallas kernels  52.9 us (97%)
  local copies, waits for them, and re-layouts  1.47 us (3%)
    pallas_call x1, Pallas kernels, dense_device(): pl.pallas_call(layer_kernel, out_shape=jax.ShapeDtypeStruct((rows, width)...  52.9 us
    unnamed x1, local copies, waits for them, and re-layouts  1.47 us

profile of v4, /device:TPU:0, one launch (start us, length us, event | category | flops | bytes accessed | tf_op | source)
XLA Modules:
  0.0 54.4 jit_solution(8452636748297551213)
XLA Ops:
  0.0 52.9 %layer.1 = bf16[32,1024]{1,0:T(8,128)(2,1)} custom-call(s32[32]{0:T(128)} %len_hbm.1, bf16[32,2048]{1,0:T(8,128)(2,1)} %q_hbm.1, bf16[32,128,128]{2,1,0:T(8,128)(2,1)} %ck_hbm.1, bf16[32,128,128]{2,1,0:T(8,128)(2,1)} %cv_hbm.1, bf16[32,128]{1,0:T(8,128)(2,1)} %nk_hbm.1, bf16[32,128]{1,0:T(8,128)(2,1)} %nv_hbm.1, bf16[2048,1024]{1,0:T(8,128)(2,1)} %wo_hbm.1, ...), custom_call_target="tpu_custom_call" | custom-call | tf_op jit(solution)/shard_map/layer/pallas_call | solution.py:540
  52.9 1.5 %copy.16 = bf16[32,1024]{1,0:T(8,128)(2,1)} copy(bf16[32,1024]{1,0:T(8,128)(2,1)} %layer.1) | data formatting | bytes 131072
